TPU v7x, 1024 devices: a whole 8x8x8 slice. The times are simulated.
1024 devices in a mesh: edp: 16 (over z, core), ep: 64 (over y, x).
Axes of the slice: x: 8, y: 8, z: 8, core: 2. Of those that a mesh axis runs over, the one named last changes fastest.
Arguments:
- tokens: bfloat16 [8192, 4096], P('ep', 'edp'), may hold values from -16 to 16
- router_weight: bfloat16 [4096, 64], P('edp'), may hold values from -0.09375 to 0.09375
- expert_ids: int32 [8192, 8], P('ep'), may hold values from 0 to 63, all different within a row; in each aligned block of 128 rows (0 to 127, 128 to 255, ...) at most 24 rows name the same one
- down_weight: bfloat16 [64, 768, 4096], P('ep', None, 'edp'), may hold values from -0.21875 to 0.21875
- expert_hidden: bfloat16 [64, 1536, 768], P('ep'), may hold values from -6 to 6
- out_grad: bfloat16 [8192, 4096], P('ep', 'edp'), may hold values from -2 to 2
Outputs:
- grad_down: float32 [64, 4096, 768], P('ep', 'edp')
- grad_hidden: bfloat16 [64, 1536, 768], P('ep', 'edp')
- grad_router: float32 [4096, 64], P(('edp', 'ep'))
- grad_tokens: bfloat16 [8192, 4096], P('ep', 'edp')
Inputs may be any that keep to these rules, and one draw needn't show every extreme that they name: `expert_ids`: each token names 8 different experts; the 128 tokens of one ep index name any one expert at most 24 times, and in every draw some ep index names some expert exactly 24 times.
All inputs are finite; a program needn't handle non-finite values.
Results may differ from a plain program's by a relative error of at most 0.0049.
Values may be sent and summed in bfloat16 or wider, within the bound.
A program may use at most 32 MiB of HBM per device.

v0:
```python
import jax
import jax.numpy as jnp
from jax import lax
from jax.sharding import PartitionSpec as P


def per_device(tokens, router_weight, expert_ids, down_weight, expert_hidden, out_grad):
    tok_rows, block_width = tokens.shape
    top_picks = expert_ids.shape[1]
    expert_count = router_weight.shape[1]
    ep_size = lax.axis_size("ep")
    edp_size = lax.axis_size("edp")
    slot_total = expert_hidden.shape[1]
    capacity = slot_total // ep_size
    share = slot_total // edp_size
    my_start = lax.axis_index("edp") * share
    partial_logits = jnp.dot(tokens, router_weight, preferred_element_type=jnp.float32)
    logits = lax.psum(partial_logits, "edp")
    expert_range = jnp.arange(expert_count, dtype=jnp.int32)
    selector = (expert_ids[:, :, None] == expert_range).astype(jnp.float32)
    picked = jnp.sum(selector * logits[:, None, :], axis=2)
    raised = jnp.exp(picked)
    route_probs = raised / jnp.sum(raised, axis=1, keepdims=True)
    sent_probs = route_probs.astype(jnp.bfloat16)
    flat_ids = expert_ids.reshape(-1)
    counted = (flat_ids[:, None] == expert_range).astype(jnp.int32)
    slot_rank = jnp.sum((jnp.cumsum(counted, axis=0) - 1) * counted, axis=1)
    position = flat_ids * capacity + slot_rank
    placed_float = (position[None, :] == jnp.arange(slot_total, dtype=jnp.int32)[:, None]).astype(
        jnp.float32
    )
    token_place = jnp.sum(placed_float.reshape(slot_total, tok_rows, top_picks), axis=2).astype(
        jnp.bfloat16
    )
    send_grad = jnp.dot(token_place, out_grad, preferred_element_type=jnp.float32).astype(
        jnp.bfloat16
    )
    send_probs = jnp.sum(
        placed_float * sent_probs.reshape(-1).astype(jnp.float32)[None, :], axis=1
    ).astype(jnp.bfloat16)
    recv_grad, recv_probs = (
        lax.all_to_all(
            send_grad.reshape(ep_size, capacity, block_width),
            "ep",
            split_axis=0,
            concat_axis=0,
            tiled=True,
        ),
        lax.all_to_all(
            send_probs.reshape(ep_size, capacity), "ep", split_axis=0, concat_axis=0, tiled=True
        ),
    )
    recv_grad = recv_grad.reshape(slot_total, block_width)
    recv_probs = recv_probs.reshape(slot_total, 1).astype(jnp.float32)
    weight = down_weight[0]
    hidden_rows = expert_hidden[0]
    scaled = (recv_probs * recv_grad.astype(jnp.float32)).astype(jnp.bfloat16)
    grad_block = lax.dot_general(
        scaled, hidden_rows, (((0,), (0,)), ((), ())), preferred_element_type=jnp.float32
    )
    back_share = lax.psum_scatter(
        lax.dot_general(
            recv_grad, weight, (((1,), (1,)), ((), ())), preferred_element_type=jnp.float32
        ),
        "edp",
        scatter_dimension=0,
        tiled=True,
    )
    my_probs = lax.dynamic_slice_in_dim(recv_probs, my_start, share, 0)
    hidden_grad = (my_probs * back_share).astype(jnp.bfloat16)[None]
    output_block = jnp.dot(hidden_rows, weight, preferred_element_type=jnp.float32)
    partial_scores = jnp.sum(output_block * recv_grad.astype(jnp.float32), axis=1)
    slot_scores = lax.psum(partial_scores, "edp")
    returned = lax.all_to_all(
        slot_scores.reshape(ep_size, capacity), "ep", split_axis=0, concat_axis=0, tiled=True
    ).reshape(slot_total)
    pick_scores = jnp.sum(placed_float * returned[:, None], axis=0).reshape(tok_rows, top_picks)
    centered = route_probs * (
        pick_scores - jnp.sum(route_probs * pick_scores, axis=1, keepdims=True)
    )
    logit_grad = jnp.sum(selector * centered[:, :, None], axis=1)
    grad_tokens = lax.dot_general(
        logit_grad,
        router_weight.astype(jnp.float32),
        (((1,), (1,)), ((), ())),
        precision=lax.Precision.HIGHEST,
        preferred_element_type=jnp.float32,
    ).astype(jnp.bfloat16)
    tokens_wide = tokens.astype(jnp.float32)
    grad_router = lax.psum_scatter(
        lax.dot_general(
            tokens_wide,
            logit_grad,
            (((0,), (0,)), ((), ())),
            precision=lax.Precision.HIGHEST,
            preferred_element_type=jnp.float32,
        ),
        "ep",
        scatter_dimension=0,
        tiled=True,
    )
    return (grad_block[None], hidden_grad, grad_router, grad_tokens)


def solution(mesh):
    in_specs = (
        P("ep", "edp"),
        P("edp", None),
        P("ep", None),
        P("ep", None, "edp"),
        P("ep", None, None),
        P("ep", "edp"),
    )
    out_specs = (P("ep", "edp", None), P("ep", "edp", None), P(("edp", "ep"), None), P("ep", "edp"))
    return jax.shard_map(
        per_device, mesh=mesh, in_specs=in_specs, out_specs=out_specs, check_vma=False
    )
```

profile of v0, /device:TPU:1, one launch (start us, length us, event | category | flops | bytes accessed | tf_op | source)
XLA Modules:
  0.0 324.4 jit_solution(14787248263341599652)
XLA Ops:
  8.0 0.9 copy.51
  9.0 0.1 eq.59
  9.1 0.1 reshape.164
  9.2 18.0 %reduce-window.6 = s32[64,8,128]{2,1,0:T(8,128)S(1)} reduce-window(s32[64,8,128]{2,1,0:T(8,128)S(1)} %fusion.15, s32[]{:T(128)} %constant.20.clone.1), window={size=1x1x128 pad=0_0x0_0x127_0}, to_apply=%region_0.0 | reduce-window | flops 8323072 | bytes 524292 | tf_op jit(solution)/shard_map/reduce-window
  27.2 0.1 slice.8
  27.3 0.1 copy.53
  27.5 0.1 copy.54
  27.6 0.1 add_add_fusion
  27.8 0.1 reduce_sum.87
  28.0 8.1 %convert_reduce_fusion = bf16[1536,128]{1,0:T(8,128)(2,1)S(1)} fusion(s32[128,8]{0,1:T(8,128)S(1)} %multiply_add_fusion), kind=kLoop, calls=%fused_computation.1 | loop fusion | flops 4521984 | bytes 397312 | tf_op jit(solution)/shard_map/reduce_sum | solution.py:32
  36.0 1.2 convolution_convert_fusion
  37.3 14.0 %all-to-all-start.1 = ((bf16[64,24,256]{2,1,0:T(8,128)(2,1)}), bf16[64,24,256]{2,1,0:T(8,128)(2,1)S(1)}, u32[]{:S(2)}, u32[]{:S(2)}) async-start(bf16[64,24,256]{2,1,0:T(8,128)(2,1)} %bitcast.56), calls=%async_computation.1 | async-start | bytes 1572864 | tf_op jit(solution)/shard_map/all_to_all | solution.py:42
  51.3 0.6 multiply_add_fusion.1
  51.9 1.6 fusion.17
  53.5 16.6 %all-to-all-done.1 = bf16[64,24,256]{2,1,0:T(8,128)(2,1)S(1)} async-done(((bf16[64,24,256]{2,1,0:T(8,128)(2,1)}), bf16[64,24,256]{2,1,0:T(8,128)(2,1)S(1)}, u32[]{:S(2)}, u32[]{:S(2)}) %all-to-all-start.1) | async-done | bytes 786464 | tf_op jit(solution)/shard_map/all_to_all | solution.py:42
  70.1 1.2 copy.58
  71.3 2.0 fusion.3
  73.3 0.7 all_to_all.15
  74.0 62.3 %all-reduce.1 = (f32[64,1,24]{2,0,1:T(8,128)}, f32[128,64]{0,1:T(8,128)}) all-reduce(f32[64,1,24]{2,0,1:T(8,128)} %all_to_all.15, f32[128,64]{0,1:T(8,128)} %fusion.17), channel_id=1, replica_groups=mesh['edp'=16,'ep'=64] {'edp'}, use_global_device_ids=true, to_apply=%region_10.11 | all-reduce | flops 9728 | bytes 77824 | tf_op jit(solution)/shard_map/psum | solution.py:73
  136.2 0.8 select_reduce_fusion.3
  137.1 7.5 %all-to-all-start.2 = ((f32[64,1,24]{2,1,0:T(1,128)}), f32[64,1,24]{2,1,0:T(1,128)}, u32[]{:S(2)}, u32[]{:S(2)}) async-start(f32[64,1,24]{2,1,0:T(1,128)} %bitcast.60), calls=%async_computation.3 | async-start | bytes 65536 | tf_op jit(solution)/shard_map/all_to_all | solution.py:74
  144.6 0.7 copy.55
  145.4 1.5 reshape.169
  146.9 8.4 %all-to-all-done.2 = f32[64,1,24]{2,1,0:T(1,128)} async-done(((f32[64,1,24]{2,1,0:T(1,128)}), f32[64,1,24]{2,1,0:T(1,128)}, u32[]{:S(2)}, u32[]{:S(2)}) %all-to-all-start.2) | async-done | bytes 6176 | tf_op jit(solution)/shard_map/all_to_all | solution.py:74
  155.3 0.5 broadcast.87
  155.8 2.1 reduce.7
  157.9 0.8 mul.103
  158.7 2.9 select_reduce_fusion
  161.6 1.4 reshape.168
  163.0 0.9 copy.61
  163.9 0.7 multiply_reduce_fusion
  164.6 0.7 subtract_multiply_fusion
  165.3 0.6 copy-done.2
  166.0 1.6 convolution_bitcast_fusion
  167.7 2.9 fusion.10
  170.7 1.3 dynamic-slice
  172.6 0.7 convert_element_type.112
  173.3 4.6 %all-to-all-start = ((bf16[64,1,24]{2,1,0:T(2,128)(2,1)}), bf16[64,1,24]{2,1,0:T(2,128)(2,1)S(1)}, u32[]{:S(2)}, u32[]{:S(2)}) async-start(bf16[64,1,24]{2,1,0:T(2,128)(2,1)} %convert_element_type.112), calls=%async_computation | async-start | bytes 65536 | tf_op jit(solution)/shard_map/all_to_all | solution.py:49
  177.9 0.9 convolution_convert_fusion.1
  178.8 9.9 %all-to-all-done = bf16[64,1,24]{2,1,0:T(2,128)(2,1)S(1)} async-done(((bf16[64,1,24]{2,1,0:T(2,128)(2,1)}), bf16[64,1,24]{2,1,0:T(2,128)(2,1)S(1)}, u32[]{:S(2)}, u32[]{:S(2)}) %all-to-all-start) | async-done | bytes 3104 | tf_op jit(solution)/shard_map/all_to_all | solution.py:49
  188.7 0.1 convert_reduce_fusion.1
  188.8 0.1 reshape.171
  189.0 0.3 multiply_convert_fusion
  189.3 1.7 fusion.6
  191.0 122.8 %all-reduce.4.cloned.1.call-done = f32[256,64]{0,1:T(8,128)} async-done(((f32[256,64]{0,1:T(8,128)}), f32[256,64]{0,1:T(8,128)}) %all-reduce.4.cloned.1.call-update) | async-done | bytes 65552
  313.8 0.8 constant_dynamic-slice_fusion
  314.6 0.7 copy.62
  315.3 1.7 fusion.16
  (33 shorter events, 0.5 us)
Async XLA Ops:
  8.0 63.3 %copy-start = (bf16[1,1536,768]{2,1,0:T(8,128)(2,1)S(1)}, bf16[1,1536,768]{2,1,0:T(8,128)(2,1)}, u32[]{:S(2)}) copy-start(bf16[1,1536,768]{2,1,0:T(8,128)(2,1)} %param.10) | copy-start | bytes 7077892
  8.0 19.9 %copy-start.6 = (s32[128,8]{0,1:T(8,128)S(1)}, s32[128,8]{0,1:T(8,128)}, u32[]{:S(2)}) copy-start(s32[128,8]{0,1:T(8,128)} %param.8) | copy-start | bytes 12292
  8.0 28.0 %copy-start.5 = (bf16[128,256]{1,0:T(8,128)(2,1)S(1)}, bf16[128,256]{1,0:T(8,128)(2,1)}, u32[]{:S(2)}) copy-start(bf16[128,256]{1,0:T(8,128)(2,1)} %param.11) | copy-start | bytes 196612
  36.0 35.3 %copy-start.1 = (bf16[1,768,256]{2,1,0:T(8,128)(2,1)S(1)}, bf16[1,768,256]{2,1,0:T(8,128)(2,1)}, u32[]{:S(2)}) copy-start(bf16[1,768,256]{2,1,0:T(8,128)(2,1)} %param.9) | copy-start | bytes 1179652
  37.3 32.9 %all-to-all-start.1 = ((bf16[64,24,256]{2,1,0:T(8,128)(2,1)}), bf16[64,24,256]{2,1,0:T(8,128)(2,1)S(1)}, u32[]{:S(2)}, u32[]{:S(2)}) async-start(bf16[64,24,256]{2,1,0:T(8,128)(2,1)} %bitcast.56), calls=%async_computation.1 | async-start | bytes 1572864 | tf_op jit(solution)/shard_map/all_to_all | solution.py:42
  137.0 18.7 %copy-start.7 = (f32[128]{0:T(128)}, f32[128]{0:T(128)S(1)}, u32[]{:S(2)}) copy-start(f32[128]{0:T(128)S(1)} %exponential_reduce_fusion) | copy-start | bytes 1540
  137.1 18.2 %all-to-all-start.2 = ((f32[64,1,24]{2,1,0:T(1,128)}), f32[64,1,24]{2,1,0:T(1,128)}, u32[]{:S(2)}, u32[]{:S(2)}) async-start(f32[64,1,24]{2,1,0:T(1,128)} %bitcast.60), calls=%async_computation.3 | async-start | bytes 65536 | tf_op jit(solution)/shard_map/all_to_all | solution.py:74
  144.6 169.2 %all-reduce.4.cloned.1.call-start = ((), (), s32[]{:S(2)}) async-start(), calls=%async_computation.5 | async-start | bytes 131072
  165.3 0.6 copy-start.2
  167.6 147.7 %reduce-scatter.3.cloned.1.call-start = ((), (), s32[]{:S(2)}) async-start(), calls=%async_computation.4 | async-start | bytes 5013504 | tf_op jit(solution)/shard_map/reduce_scatter | solution.py:61
  170.6 2.0 copy-start.8
  170.6 7.3 %copy-start.3 = (f32[128,64]{0,1:T(8,128)S(1)}, f32[128,64]{0,1:T(8,128)}, u32[]{:S(2)}) copy-start(f32[128,64]{0,1:T(8,128)} %copy-done.2) | copy-start | bytes 98308
  170.6 7.3 %copy-start.4 = (bf16[256,64]{0,1:T(8,128)(2,1)S(1)}, bf16[256,64]{0,1:T(8,128)(2,1)}, u32[]{:S(2)}) copy-start(bf16[256,64]{0,1:T(8,128)(2,1)} %param.7) | copy-start | bytes 98308
  173.3 15.4 %all-to-all-start = ((bf16[64,1,24]{2,1,0:T(2,128)(2,1)}), bf16[64,1,24]{2,1,0:T(2,128)(2,1)S(1)}, u32[]{:S(2)}, u32[]{:S(2)}) async-start(bf16[64,1,24]{2,1,0:T(2,128)(2,1)} %convert_element_type.112), calls=%async_computation | async-start | bytes 65536 | tf_op jit(solution)/shard_map/all_to_all | solution.py:49
Sparse Core Ops, SparseCore 0:
  167.7 146.0 all-reduce.3
Sparse Core Ops, SparseCore 1:
  171.5 59.4 reduce-scatter.2
where the time goes:
time: 329 us; the launch traced here: 324 us
  waiting for transfers between devices  158 us (48%)
  blocking collectives  62.3 us (19%)
  other arithmetic  36.2 us (11%)
  starting transfers between devices  26.2 us (8%)
  between operations  16.4 us (5%)
  local copies, waits for them, and re-layouts  13.6 us (4%)
  matrix products  12 us (4%)
    unnamed x3, waiting for transfers between devices  123 us
    psum x1, blocking collectives, per_device(): slot_scores = lax.psum(partial_scores, 'edp')  62.3 us
    another operation x2, other arithmetic  18 us
    all_to_all x1, waiting for transfers between devices, per_device(): lax.all_to_all(send_grad.reshape(ep_size, capacity, block_width), 'ep', s...  16.6 us
    all_to_all x1, starting transfers between devices, per_device(): lax.all_to_all(send_grad.reshape(ep_size, capacity, block_width), 'ep', s...  14 us
    all_to_all x1, waiting for transfers between devices, per_device(): lax.all_to_all(send_probs.reshape(ep_size, capacity), 'ep', split_axis=0,...  9.87 us
    all_to_all x1, waiting for transfers between devices, per_device(): lax.all_to_all(slot_scores.reshape(ep_size, capacity), 'ep', split_axis=0...  8.38 us
    reduce_sum x1, other arithmetic, per_device(): jnp.sum(placed_float.reshape(slot_total, tok_rows, top_picks), axis=2)  8.05 us
  transfers between devices with their start and end apart: 5, of which 4 were waited for; matrix products, arithmetic and copies ran while one was open for 4% of the time, Pallas kernels for 0%

commit v1 on v0

v1 whole, which is shorter than its diff:
```python
import functools
import math

import jax
import jax.numpy as jnp
from jax import lax
from jax.experimental import pallas as pl
from jax.experimental.pallas import tpu as pltpu
from jax.sharding import PartitionSpec as P

F32 = jnp.float32
BF16 = jnp.bfloat16
NN = (((1,), (0,)), ((), ()))
NT = (((1,), (1,)), ((), ()))
TN = (((0,), (0,)), ((), ()))


def matmul(a, b, dims):
    return lax.dot_general(a, b, dims, preferred_element_type=F32)


def split(a):
    high = a.astype(BF16)
    rest = a - high.astype(F32)
    middle = rest.astype(BF16)
    return high, middle, (rest - middle.astype(F32)).astype(BF16)


def push(src, dst, send, recv, device):
    pltpu.make_async_remote_copy(
        src_ref=src,
        dst_ref=dst,
        send_sem=send,
        recv_sem=recv,
        device_id=device,
        device_id_type=pl.DeviceIdType.MESH,
    ).start()


def drain(ref, sem):
    pltpu.make_async_copy(ref, ref, sem).wait()


def kernel(
    side,
    cap,
    tok,
    rwt,
    idt,
    w_any,
    h_any,
    grad,
    down_o,
    hid_o,
    router_o,
    gtok_o,
    w,
    h,
    rank_s,
    gsend,
    grecv,
    psend,
    precv,
    ysend,
    yrecv,
    lsend,
    lrecv,
    fsend,
    frecv,
    back_s,
    own,
    own_total,
    xsend,
    xrecv,
    zsend,
    zrecv,
    pcol_s,
    scaled,
    rsend,
    rrecv,
    load_sem,
    l_sem,
    g_send,
    g_recv,
    p_send,
    p_recv,
    y_sem,
    f_sem,
    x_send,
    x_recv,
    z_sem,
    r_sem,
):
    q, e = lax.axis_index("edp"), lax.axis_index("ep")
    z, c = q // 2, q % 2
    y, x = e // side, e % side
    ep, edp = lax.axis_size("ep"), lax.axis_size("edp")
    rows = ep // side
    top, count = idt.shape
    width = tok.shape[1]
    group = side * cap
    share = group // 2

    load_w = pltpu.make_async_copy(w_any, w, load_sem.at[0])
    load_h = pltpu.make_async_copy(h_any, h, load_sem.at[1])
    load_w.start()
    load_h.start()

    barrier = pltpu.get_barrier_semaphore()

    @pl.loop(1, ep)
    def _(i):
        pl.semaphore_signal(
            barrier, inc=1, device_id=(q, (e + i) % ep), device_id_type=pl.DeviceIdType.MESH
        )

    @pl.loop(1, edp)
    def _(i):
        pl.semaphore_signal(
            barrier, inc=1, device_id=((q + i) % edp, e), device_id_type=pl.DeviceIdType.MESH
        )

    expert = lax.broadcasted_iota(jnp.int32, (ep, count), 0)
    slot = lax.broadcasted_iota(jnp.int32, (side, cap, count), 1).astype(F32)

    def select(k, values):
        return jnp.where(idt[k : k + 1, :] == expert, values, 0.0)

    def to_picks(values):
        return jnp.concatenate(
            [jnp.sum(select(k, values), axis=0, keepdims=True) for k in range(top)], axis=0
        )

    def to_experts(values):
        return sum(select(k, values[k : k + 1, :]) for k in range(top))

    def placement(ranks):
        spread = jnp.broadcast_to(ranks[:, None, :], (side, cap, count))
        return jnp.where(spread == slot, 1.0, 0.0).astype(F32).reshape(group, count)

    lsend[...] = to_picks(matmul(rwt[...], tok[...], NT))
    lrecv[q] = lsend[...]
    named = to_experts(jnp.ones((top, count), F32))
    before = (
        lax.broadcasted_iota(jnp.int32, (count, count), 0)
        < lax.broadcasted_iota(jnp.int32, (count, count), 1)
    ).astype(F32)
    rank = jnp.where(
        named > 0.0, matmul(named.astype(BF16), before.astype(BF16), NN), -1.0
    )
    rank_s[...] = rank

    pl.semaphore_wait(barrier, ep - 1 + edp - 1)

    @pl.loop(1, edp)
    def _(i):
        push(lsend, lrecv.at[q], l_sem.at[0], l_sem.at[1], ((q + i) % edp, e))

    def exchange(row, src, dst, send, recv):
        @pl.loop(0, side)
        def _(dx):
            other = row * side + (x + dx) % side

            @pl.when(other == e)
            def _():
                pltpu.make_async_copy(src.at[other], dst.at[e], recv).start()

            @pl.when(other != e)
            def _():
                push(src.at[other], dst.at[e], send, recv, (q, other))

    def offset(i):
        return (i - z + rows) % rows

    @pl.loop(0, rows)
    def _(i):
        row = (y + offset(i)) % rows
        first = pl.multiple_of(row * side, side)
        place = placement(rank_s[pl.ds(first, side), :]).astype(BF16)
        picked = matmul(place, grad[...], NN)
        gsend[pl.ds(first, side)] = picked.reshape(side, cap, width).astype(BF16)
        exchange(row, gsend, grecv, g_send, g_recv.at[i])

    drain(lrecv.at[pl.ds(0, edp - 1)], l_sem.at[1])
    raised = jnp.exp(sum(lrecv[j] for j in range(edp)))
    probs = raised / jnp.sum(raised, axis=0, keepdims=True)
    sent = to_experts(probs.astype(BF16).astype(F32))
    psend[:, 0, :] = jnp.concatenate([sent, rank], axis=1)

    @pl.loop(0, rows)
    def _(i):
        exchange((y + offset(i)) % rows, psend, precv, p_send, p_recv.at[i])

    load_w.wait()
    load_h.wait()

    def forward(i):
        row = (y - offset(i) + rows) % rows
        drain(xrecv.at[i], x_recv.at[i])
        total = own[i] + xrecv[i].astype(F32)

        @pl.when(row == z)
        def _():
            own_total[...] = total

        @pl.when(row != z)
        def _():
            zsend[i] = total.astype(BF16)
            push(zsend.at[i], zrecv.at[z], z_sem.at[0], z_sem.at[1], (row * 2 + c, e))

    @pl.loop(0, rows)
    def _(i):
        row = (y - offset(i) + rows) % rows
        first = pl.multiple_of(row * side, side)
        start = pl.multiple_of(row * group, group)
        drain(grecv.at[pl.ds(first, side)], g_recv.at[i])
        drain(precv.at[pl.ds(first, side)], p_recv.at[i])
        wide = grecv[pl.ds(first, side)].astype(F32).reshape(group, width)
        back = matmul(wide.astype(BF16), w[...], NT)
        back_s[...] = back
        xsend[i] = back_s[pl.ds(pl.multiple_of((1 - c) * share, share), share), :].astype(BF16)
        push(xsend.at[i], xrecv.at[i], x_send, x_recv.at[i], (z * 2 + 1 - c, e))
        own[i] = back_s[pl.ds(pl.multiple_of(c * share, share), share), :]

        met = precv[pl.ds(first, side), 0, :]
        place = placement(met[:, count:])
        spread = jnp.broadcast_to(met[:, None, :count], (side, cap, count))
        pcol = jnp.sum(place * spread.reshape(group, count), axis=1, keepdims=True)
        score = jnp.sum(back * h[pl.ds(start, group), :].astype(F32), axis=1, keepdims=True)
        ysend[pl.ds(first, side), 0, :] = jnp.sum(
            (place * score).reshape(side, cap, count), axis=1
        )
        exchange(row, ysend, yrecv, y_sem.at[0], y_sem.at[1])
        scaled[pl.ds(start, group), :] = (pcol * wide).astype(BF16)

        @pl.when(row == z)
        def _():
            pcol_s[...] = jnp.broadcast_to(pcol, pcol_s.shape)

        @pl.when(i > 0)
        def _():
            forward(i - 1)

    forward(rows - 1)

    drain(yrecv, y_sem.at[1])
    fsend[...] = to_picks(yrecv[:, 0, :])
    frecv[q] = fsend[...]

    @pl.loop(1, edp)
    def _(i):
        push(fsend, frecv.at[q], f_sem.at[0], f_sem.at[1], ((q + i) % edp, e))

    down_o[...] = matmul(scaled[...], h[...], TN)
    wanted = lax.broadcasted_iota(jnp.int32, (width, width), 0)
    wanted = (wanted % ep) * (width // ep) + wanted // ep
    order = (wanted == lax.broadcasted_iota(jnp.int32, (width, width), 1)).astype(F32)
    turned = matmul(order.astype(BF16), tok[...], NT).astype(BF16)

    drain(frecv.at[pl.ds(0, edp - 1)], f_sem.at[1])
    scores = sum(frecv[j] for j in range(edp))
    centered = probs * (scores - jnp.sum(probs * scores, axis=0, keepdims=True))
    parts = split(to_experts(centered))

    terms = sum(matmul(turned, part, NT) for part in parts)
    rsend[:, 0, :] = jnp.concatenate(
        [terms[j * ep : (j + 1) * ep, :] for j in range(width // ep)], axis=1
    )

    @pl.loop(0, rows)
    def _(i):
        exchange((y + offset(i)) % rows, rsend, rrecv, r_sem.at[0], r_sem.at[1])

    gtok_o[...] = sum(matmul(part, rwt[...], TN) for part in parts).astype(BF16)

    drain(zrecv.at[pl.ds(0, rows - 1)], z_sem.at[1])
    total = own_total[...]
    for j in range(1, rows):
        total = total + zrecv[(z + j) % rows].astype(F32)
    mine = pcol_s[pl.ds(pl.multiple_of(c * share, share), share), :]
    hid_o[...] = (total * mine[:, :1]).astype(BF16)

    drain(rrecv, r_sem.at[1])
    line = jnp.sum(rrecv[...], axis=0)
    for j in range(width // ep):
        router_o[j : j + 1, :] = line[:, j * ep : (j + 1) * ep]

    drain(lrecv.at[pl.ds(0, edp - 1)], l_sem.at[0])
    drain(frecv.at[pl.ds(0, edp - 1)], f_sem.at[0])
    drain(gsend.at[pl.ds(0, ep - 1)], g_send)
    drain(psend.at[pl.ds(0, ep - 1)], p_send)
    drain(ysend.at[pl.ds(0, ep - 1)], y_sem.at[0])
    drain(xsend, x_send)
    drain(zsend.at[pl.ds(0, rows - 1)], z_sem.at[0])
    drain(rsend.at[pl.ds(0, ep - 1)], r_sem.at[0])


def per_device(tokens, router_weight, expert_ids, down_weight, expert_hidden, out_grad):
    count, width = tokens.shape
    top = expert_ids.shape[1]
    ep, edp = lax.axis_size("ep"), lax.axis_size("edp")
    side = math.isqrt(ep)
    rows = ep // side
    slots, ffw = expert_hidden.shape[1:]
    cap = slots // ep
    group = side * cap
    share = slots // edp
    dma = pltpu.SemaphoreType.DMA
    vmem = pl.BlockSpec(memory_space=pltpu.VMEM)
    any_ = pl.BlockSpec(memory_space=pl.ANY)
    down, hidden, router, gtok = pl.pallas_call(
        functools.partial(kernel, side, cap),
        out_shape=(
            jax.ShapeDtypeStruct((width, ffw), F32),
            jax.ShapeDtypeStruct((share, ffw), BF16),
            jax.ShapeDtypeStruct((width // ep, ep), F32),
            jax.ShapeDtypeStruct((count, width), BF16),
        ),
        in_specs=[vmem, vmem, vmem, any_, any_, vmem],
        out_specs=(vmem, vmem, vmem, vmem),
        scratch_shapes=[
            pltpu.VMEM((ffw, width), BF16),
            pltpu.VMEM((slots, ffw), BF16),
            pltpu.VMEM((ep, count), F32),
            pltpu.VMEM((ep, cap, width), BF16),
            pltpu.VMEM((ep, cap, width), BF16),
            pltpu.VMEM((ep, 1, 2 * count), F32),
            pltpu.VMEM((ep, 1, 2 * count), F32),
            pltpu.VMEM((ep, 1, count), F32),
            pltpu.VMEM((ep, 1, count), F32),
            pltpu.VMEM((top, count), F32),
            pltpu.VMEM((edp, top, count), F32),
            pltpu.VMEM((top, count), F32),
            pltpu.VMEM((edp, top, count), F32),
            pltpu.VMEM((group, ffw), F32),
            pltpu.VMEM((rows, share, ffw), F32),
            pltpu.VMEM((share, ffw), F32),
            pltpu.VMEM((rows, share, ffw), BF16),
            pltpu.VMEM((rows, share, ffw), BF16),
            pltpu.VMEM((rows, share, ffw), BF16),
            pltpu.VMEM((rows, share, ffw), BF16),
            pltpu.VMEM((group, 128), F32),
            pltpu.VMEM((slots, width), BF16),
            pltpu.VMEM((ep, 1, width), F32),
            pltpu.VMEM((ep, 1, width), F32),
            dma((2,)),
            dma((2,)),
            dma,
            dma((rows,)),
            dma,
            dma((rows,)),
            dma((2,)),
            dma((2,)),
            dma,
            dma((rows,)),
            dma((2,)),
            dma((2,)),
        ],
        compiler_params=pltpu.CompilerParams(
            collective_id=0, has_side_effects=True, vmem_limit_bytes=48 * 1024 * 1024
        ),
    )(tokens, router_weight.T, expert_ids.T, down_weight[0], expert_hidden[0], out_grad)
    return down[None], hidden[None], router, gtok


def solution(mesh):
    in_specs = (
        P("ep", "edp"),
        P("edp", None),
        P("ep", None),
        P("ep", None, "edp"),
        P("ep", None, None),
        P("ep", "edp"),
    )
    out_specs = (P("ep", "edp", None), P("ep", "edp", None), P(("edp", "ep"), None), P("ep", "edp"))
    return jax.shard_map(
        per_device, mesh=mesh, in_specs=in_specs, out_specs=out_specs, check_vma=False
    )
```

time: 329 us -> 114 us (0.35); the launches traced: 324 us -> 113 us
  waiting for transfers between devices: 158 us -> 0 us
  Pallas kernels: 0 us -> 104 us
  blocking collectives: 62.3 us -> 0 us
  other arithmetic: 36.2 us -> 0 us
  starting transfers between devices: 26.2 us -> 0 us
  between operations: 16.4 us -> 0.66 us
  matrix products: 12 us -> 0 us
  local copies, waits for them, and re-layouts: 13.6 us -> 8.52 us
    unnamed x3 -> x0, waiting for transfers between devices: 123 us -> none
    pallas_call x0 -> x1, Pallas kernels: none -> 104 us  [per_device(): pl.pallas_call(functools.partial(kernel, side, cap), out_shape=(jax.Shape...]
    psum x1 -> x0, blocking collectives: 62.3 us -> none  [per_device(): slot_scores = lax.psum(partial_scores, 'edp')]
    all_to_all x3 -> x0, waiting for transfers between devices: 34.9 us -> none  [the longest x1 16.6 us: per_device(): lax.all_to_all(send_grad.reshape(ep_size, capacity, block_width), 'ep', s...]
    all_to_all x3 -> x0, starting transfers between devices: 26.1 us -> none  [the longest x1 14 us: per_device(): lax.all_to_all(send_grad.reshape(ep_size, capacity, block_width), 'ep', s...]
    another operation x2 -> x0, other arithmetic: 18 us -> none
    reduce_sum x7 -> x0, other arithmetic: 12.6 us -> none  [the longest x1 8.05 us: per_device(): jnp.sum(placed_float.reshape(slot_total, tok_rows, top_picks), axis=2)]
    dot_general x7 -> x0, matrix products: 12 us -> none  [the longest x1 2.94 us: per_device(): lax.dot_general(recv_grad, weight, (((1,), (1,)), ((), ())), preferred_el...]
  transfers between devices with their start and end apart: 5 -> 0, of which waited for: 4 -> 0; matrix products, arithmetic and copies ran while one was open for 4% -> 0% of each run, Pallas kernels for 0% -> 0%
where the time goes in v1:
time: 114 us; the launch traced here: 113 us
  Pallas kernels  104 us (91%)
  local copies, waits for them, and re-layouts  8.52 us (7%)
    pallas_call x1, Pallas kernels, per_device(): pl.pallas_call(functools.partial(kernel, side, cap), out_shape=(jax.Shape...  104 us
    unnamed x16, local copies, waits for them, and re-layouts  8.52 us

profile of v1, /device:TPU:1, one launch (start us, length us, event | category | flops | bytes accessed | tf_op | source)
XLA Modules:
  0.0 113.2 jit_solution(16417475056695276739)
XLA Ops:
  0.6 0.0 copy-start
  0.6 1.7 %copy-done = bf16[1,1536,768]{2,1,0:T(8,128)(2,1)S(1)} copy-done((bf16[1,1536,768]{2,1,0:T(8,128)(2,1)S(1)}, bf16[1,1536,768]{2,1,0:T(8,128)(2,1)}, u32[]{:S(2)}) %copy-start) | copy-done | bytes 2359320
  2.3 0.0 copy-start.1
  2.3 1.0 copy-done.1
  3.3 0.0 copy-start.2
  3.3 0.8 copy-done.2
  4.1 0.0 copy-start.3
  4.1 0.8 copy-done.3
  5.0 0.0 copy-start.4
  5.0 0.8 copy-done.4
  5.7 0.0 copy-start.5
  5.7 0.7 copy-done.5
  6.4 104.0 %shard_map.93 = (f32[256,768]{1,0:T(8,128)S(1)}, bf16[96,768]{1,0:T(8,128)(2,1)S(1)}, f32[4,64]{1,0:T(4,128)S(1)}, bf16[128,256]{1,0:T(8,128)(2,1)S(1)}) custom-call(bf16[128,256]{1,0:T(8,128)(2,1)S(1)} %copy-done.2, bf16[64,256]{1,0:T(8,128)(2,1)S(1)} %bitcast.10, s32[8,128]{1,0:T(8,128)S(1)} %bitcast.11, bf16[768,256]{1,0:T(8,128)(2,1)S(1)} %bitcast.8, ...), custom_call_target="tpu_custom_call" | custom-call | tf_op jit(solution)/shard_map/pallas_call | solution.py:311
  110.4 0.9 copy.14
  111.3 0.7 copy.15
  112.0 0.6 copy.16
  112.6 0.6 copy.17
Async XLA Ops:
  0.6 1.7 %copy-start = (bf16[1,1536,768]{2,1,0:T(8,128)(2,1)S(1)}, bf16[1,1536,768]{2,1,0:T(8,128)(2,1)}, u32[]{:S(2)}) copy-start(bf16[1,1536,768]{2,1,0:T(8,128)(2,1)} %param.10) | copy-start | bytes 7077892
  2.3 1.0 copy-start.1
  3.3 0.8 copy-start.2
  4.1 0.8 copy-start.3
  5.0 0.8 copy-start.4
  5.7 0.7 copy-start.5

commit v2 on v1

--- a/solution.py
+++ b/solution.py
@@ -13,6 +13,8 @@
 NN = (((1,), (0,)), ((), ()))
 NT = (((1,), (1,)), ((), ()))
 TN = (((0,), (0,)), ((), ()))
+EARLY = 4
+HELD = 7
 
 
 def matmul(a, b, dims):
@@ -44,22 +46,28 @@
 def kernel(
     side,
     cap,
-    tok,
-    rwt,
-    idt,
+    tok_any,
+    rwt_any,
+    idt_any,
     w_any,
     h_any,
-    grad,
+    grad_any,
     down_o,
     hid_o,
     router_o,
     gtok_o,
+    tok,
+    rwt,
+    idt,
+    grad,
     w,
     h,
     rank_s,
+    probs_s,
     gsend,
     grecv,
     psend,
+    pmid,
     precv,
     ysend,
     yrecv,
@@ -77,13 +85,14 @@
     pcol_s,
     scaled,
     rsend,
+    rmid,
+    rsum,
     rrecv,
     load_sem,
     l_sem,
     g_send,
     g_recv,
-    p_send,
-    p_recv,
+    p_sem,
     y_sem,
     f_sem,
     x_send,
@@ -101,10 +110,14 @@
     group = side * cap
     share = group // 2
 
-    load_w = pltpu.make_async_copy(w_any, w, load_sem.at[0])
-    load_h = pltpu.make_async_copy(h_any, h, load_sem.at[1])
-    load_w.start()
-    load_h.start()
+    loads = [
+        pltpu.make_async_copy(src, dst, load_sem.at[j])
+        for j, (src, dst) in enumerate(
+            [(idt_any, idt), (tok_any, tok), (rwt_any, rwt), (grad_any, grad), (w_any, w), (h_any, h)]
+        )
+    ]
+    for load in loads:
+        load.start()
 
     barrier = pltpu.get_barrier_semaphore()
 
@@ -120,8 +133,12 @@
             barrier, inc=1, device_id=((q + i) % edp, e), device_id_type=pl.DeviceIdType.MESH
         )
 
+    for load in loads[:3]:
+        load.wait()
     expert = lax.broadcasted_iota(jnp.int32, (ep, count), 0)
     slot = lax.broadcasted_iota(jnp.int32, (side, cap, count), 1).astype(F32)
+    lane = lax.broadcasted_iota(jnp.int32, (side, cap, count), 2).astype(F32)
+    own_slot = jnp.where(slot == lane, 1.0, 0.0).astype(F32).reshape(group, count)
 
     def select(k, values):
         return jnp.where(idt[k : k + 1, :] == expert, values, 0.0)
@@ -150,6 +167,7 @@
     )
     rank_s[...] = rank
 
+    loads[3].wait()
     pl.semaphore_wait(barrier, ep - 1 + edp - 1)
 
     @pl.loop(1, edp)
@@ -159,7 +177,7 @@
     def exchange(row, src, dst, send, recv):
         @pl.loop(0, side)
         def _(dx):
-            other = row * side + (x + dx) % side
+            other = row * side + (x + 3 * dx) % side
 
             @pl.when(other == e)
             def _():
@@ -170,10 +188,9 @@
                 push(src.at[other], dst.at[e], send, recv, (q, other))
 
     def offset(i):
-        return (i - z + rows) % rows
-
-    @pl.loop(0, rows)
-    def _(i):
+        return (3 * i - z + rows) % rows
+
+    def dispatch(i):
         row = (y + offset(i)) % rows
         first = pl.multiple_of(row * side, side)
         place = placement(rank_s[pl.ds(first, side), :]).astype(BF16)
@@ -181,18 +198,25 @@
         gsend[pl.ds(first, side)] = picked.reshape(side, cap, width).astype(BF16)
         exchange(row, gsend, grecv, g_send, g_recv.at[i])
 
-    drain(lrecv.at[pl.ds(0, edp - 1)], l_sem.at[1])
-    raised = jnp.exp(sum(lrecv[j] for j in range(edp)))
-    probs = raised / jnp.sum(raised, axis=0, keepdims=True)
-    sent = to_experts(probs.astype(BF16).astype(F32))
-    psend[:, 0, :] = jnp.concatenate([sent, rank], axis=1)
-
-    @pl.loop(0, rows)
-    def _(i):
-        exchange((y + offset(i)) % rows, psend, precv, p_send, p_recv.at[i])
-
-    load_w.wait()
-    load_h.wait()
+    ahead = min(EARLY, rows)
+    pl.loop(0, ahead)(dispatch)
+
+    def weigh():
+        drain(lrecv.at[pl.ds(0, edp - 1)], l_sem.at[1])
+        raised = jnp.exp(sum(lrecv[j] for j in range(edp)))
+        probs = raised / jnp.sum(raised, axis=0, keepdims=True)
+        probs_s[...] = probs
+        sent = to_experts(probs.astype(BF16).astype(F32))
+        psend[...] = jnp.concatenate([sent, rank_s[...]], axis=1).reshape(psend.shape)
+        pltpu.make_async_copy(psend.at[y], pmid.at[y], p_sem.at[1]).start()
+
+        @pl.loop(1, rows)
+        def _(j):
+            other = (y + j) % rows
+            push(psend.at[other], pmid.at[y], p_sem.at[0], p_sem.at[1], (q, other * side + x))
+
+    loads[4].wait()
+    loads[5].wait()
 
     def forward(i):
         row = (y - offset(i) + rows) % rows
@@ -214,7 +238,6 @@
         first = pl.multiple_of(row * side, side)
         start = pl.multiple_of(row * group, group)
         drain(grecv.at[pl.ds(first, side)], g_recv.at[i])
-        drain(precv.at[pl.ds(first, side)], p_recv.at[i])
         wide = grecv[pl.ds(first, side)].astype(F32).reshape(group, width)
         back = matmul(wide.astype(BF16), w[...], NT)
         back_s[...] = back
@@ -222,36 +245,47 @@
         push(xsend.at[i], xrecv.at[i], x_send, x_recv.at[i], (z * 2 + 1 - c, e))
         own[i] = back_s[pl.ds(pl.multiple_of(c * share, share), share), :]
 
-        met = precv[pl.ds(first, side), 0, :]
-        place = placement(met[:, count:])
-        spread = jnp.broadcast_to(met[:, None, :count], (side, cap, count))
-        pcol = jnp.sum(place * spread.reshape(group, count), axis=1, keepdims=True)
         score = jnp.sum(back * h[pl.ds(start, group), :].astype(F32), axis=1, keepdims=True)
         ysend[pl.ds(first, side), 0, :] = jnp.sum(
-            (place * score).reshape(side, cap, count), axis=1
+            (own_slot * score).reshape(side, cap, count), axis=1
         )
         exchange(row, ysend, yrecv, y_sem.at[0], y_sem.at[1])
-        scaled[pl.ds(start, group), :] = (pcol * wide).astype(BF16)
-
-        @pl.when(row == z)
-        def _():
-            pcol_s[...] = jnp.broadcast_to(pcol, pcol_s.shape)
-
-        @pl.when(i > 0)
+
+        @pl.when((i > 0) & (i <= HELD))
         def _():
             forward(i - 1)
 
-    forward(rows - 1)
+        @pl.when(i + ahead < rows)
+        def _():
+            dispatch(i + ahead)
+
+        @pl.when(i == rows // 2)
+        def _():
+            weigh()
 
     drain(yrecv, y_sem.at[1])
-    fsend[...] = to_picks(yrecv[:, 0, :])
+    found = yrecv[:, 0, :]
+    ranks = rank_s[...]
+    spread = sum(jnp.where(ranks == float(j), found[:, j : j + 1], 0.0) for j in range(cap))
+    fsend[...] = to_picks(spread)
     frecv[q] = fsend[...]
 
     @pl.loop(1, edp)
     def _(i):
         push(fsend, frecv.at[q], f_sem.at[0], f_sem.at[1], ((q + i) % edp, e))
 
-    down_o[...] = matmul(scaled[...], h[...], TN)
+    drain(pmid, p_sem.at[1])
+    pltpu.make_async_copy(pmid.at[:, x], precv.at[:, x], p_sem.at[3]).start()
+
+    @pl.loop(1, side)
+    def _(j):
+        other = (x + j) % side
+        push(
+            pmid.at[:, other], precv.at[:, x], p_sem.at[2], p_sem.at[3], (q, y * side + other)
+        )
+
+    pl.loop(min(HELD, rows - 1), rows)(forward)
+
     wanted = lax.broadcasted_iota(jnp.int32, (width, width), 0)
     wanted = (wanted % ep) * (width // ep) + wanted // ep
     order = (wanted == lax.broadcasted_iota(jnp.int32, (width, width), 1)).astype(F32)
@@ -259,20 +293,52 @@
 
     drain(frecv.at[pl.ds(0, edp - 1)], f_sem.at[1])
     scores = sum(frecv[j] for j in range(edp))
+    probs = probs_s[...]
     centered = probs * (scores - jnp.sum(probs * scores, axis=0, keepdims=True))
     parts = split(to_experts(centered))
 
     terms = sum(matmul(turned, part, NT) for part in parts)
-    rsend[:, 0, :] = jnp.concatenate(
+    lines = jnp.concatenate(
         [terms[j * ep : (j + 1) * ep, :] for j in range(width // ep)], axis=1
     )
+    rsend[...] = lines.reshape(rsend.shape)
+
+    @pl.loop(1, side)
+    def _(j):
+        other = (x + j) % side
+        push(rsend.at[:, other], rmid.at[x], r_sem.at[0], r_sem.at[1], (q, y * side + other))
+
+    gtok_o[...] = sum(matmul(part, rwt[...], TN) for part in parts).astype(BF16)
+
+    drain(precv, p_sem.at[3])
 
     @pl.loop(0, rows)
-    def _(i):
-        exchange((y + offset(i)) % rows, rsend, rrecv, r_sem.at[0], r_sem.at[1])
-
-    gtok_o[...] = sum(matmul(part, rwt[...], TN) for part in parts).astype(BF16)
-
+    def _(row):
+        first = pl.multiple_of(row * side, side)
+        start = pl.multiple_of(row * group, group)
+        met = precv[row].reshape(side, 2 * count)
+        place = placement(met[:, count:])
+        weights = jnp.broadcast_to(met[:, None, :count], (side, cap, count))
+        pcol = jnp.sum(place * weights.reshape(group, count), axis=1, keepdims=True)
+        wide = grecv[pl.ds(first, side)].astype(F32).reshape(group, width)
+        scaled[pl.ds(start, group), :] = (pcol * wide).astype(BF16)
+
+        @pl.when(row == z)
+        def _():
+            pcol_s[...] = jnp.broadcast_to(pcol, pcol_s.shape)
+
+    drain(rmid.at[pl.ds(0, side - 1)], r_sem.at[1])
+    line = rsend[:, x]
+    for j in range(1, side):
+        line = line + rmid[(x + j) % side]
+    rsum[...] = line
+
+    @pl.loop(1, rows)
+    def _(j):
+        other = (y + j) % rows
+        push(rsum.at[other], rrecv.at[y], r_sem.at[2], r_sem.at[3], (q, other * side + x))
+
+    down_o[...] = matmul(scaled[...], h[...], TN)
     drain(zrecv.at[pl.ds(0, rows - 1)], z_sem.at[1])
     total = own_total[...]
     for j in range(1, rows):
@@ -280,19 +346,23 @@
     mine = pcol_s[pl.ds(pl.multiple_of(c * share, share), share), :]
     hid_o[...] = (total * mine[:, :1]).astype(BF16)
 
-    drain(rrecv, r_sem.at[1])
-    line = jnp.sum(rrecv[...], axis=0)
+    drain(rrecv.at[pl.ds(0, rows - 1)], r_sem.at[3])
+    line = rsum[y]
+    for j in range(1, rows):
+        line = line + rrecv[(y + j) % rows]
     for j in range(width // ep):
         router_o[j : j + 1, :] = line[:, j * ep : (j + 1) * ep]
 
     drain(lrecv.at[pl.ds(0, edp - 1)], l_sem.at[0])
     drain(frecv.at[pl.ds(0, edp - 1)], f_sem.at[0])
     drain(gsend.at[pl.ds(0, ep - 1)], g_send)
-    drain(psend.at[pl.ds(0, ep - 1)], p_send)
+    drain(psend.at[pl.ds(0, rows - 1)], p_sem.at[0])
+    drain(pmid.at[pl.ds(0, side - 1)], p_sem.at[2])
     drain(ysend.at[pl.ds(0, ep - 1)], y_sem.at[0])
     drain(xsend, x_send)
     drain(zsend.at[pl.ds(0, rows - 1)], z_sem.at[0])
-    drain(rsend.at[pl.ds(0, ep - 1)], r_sem.at[0])
+    drain(rmid.at[pl.ds(0, side - 1)], r_sem.at[0])
+    drain(rrecv.at[pl.ds(0, rows - 1)], r_sem.at[2])
 
 
 def per_device(tokens, router_weight, expert_ids, down_weight, expert_hidden, out_grad):
@@ -308,24 +378,31 @@
     dma = pltpu.SemaphoreType.DMA
     vmem = pl.BlockSpec(memory_space=pltpu.VMEM)
     any_ = pl.BlockSpec(memory_space=pl.ANY)
+    shapes = (
+        jax.ShapeDtypeStruct((width, ffw), F32),
+        jax.ShapeDtypeStruct((share, ffw), BF16),
+        jax.ShapeDtypeStruct((width // ep, ep), F32),
+        jax.ShapeDtypeStruct((count, width), BF16),
+    )
     down, hidden, router, gtok = pl.pallas_call(
         functools.partial(kernel, side, cap),
-        out_shape=(
-            jax.ShapeDtypeStruct((width, ffw), F32),
-            jax.ShapeDtypeStruct((share, ffw), BF16),
-            jax.ShapeDtypeStruct((width // ep, ep), F32),
-            jax.ShapeDtypeStruct((count, width), BF16),
-        ),
-        in_specs=[vmem, vmem, vmem, any_, any_, vmem],
+        out_shape=shapes,
+        in_specs=[any_] * 6,
         out_specs=(vmem, vmem, vmem, vmem),
         scratch_shapes=[
+            pltpu.VMEM((count, width), BF16),
+            pltpu.VMEM((ep, width), BF16),
+            pltpu.VMEM((top, count), jnp.int32),
+            pltpu.VMEM((count, width), BF16),
             pltpu.VMEM((ffw, width), BF16),
             pltpu.VMEM((slots, ffw), BF16),
             pltpu.VMEM((ep, count), F32),
+            pltpu.VMEM((top, count), F32),
             pltpu.VMEM((ep, cap, width), BF16),
             pltpu.VMEM((ep, cap, width), BF16),
-            pltpu.VMEM((ep, 1, 2 * count), F32),
-            pltpu.VMEM((ep, 1, 2 * count), F32),
+            pltpu.VMEM((rows, side, 1, 2 * count), F32),
+            pltpu.VMEM((rows, side, 1, 2 * count), F32),
+            pltpu.VMEM((rows, side, 1, 2 * count), F32),
             pltpu.VMEM((ep, 1, count), F32),
             pltpu.VMEM((ep, 1, count), F32),
             pltpu.VMEM((top, count), F32),
@@ -341,23 +418,24 @@
             pltpu.VMEM((rows, share, ffw), BF16),
             pltpu.VMEM((group, 128), F32),
             pltpu.VMEM((slots, width), BF16),
-            pltpu.VMEM((ep, 1, width), F32),
-            pltpu.VMEM((ep, 1, width), F32),
-            dma((2,)),
+            pltpu.VMEM((rows, side, 1, width), F32),
+            pltpu.VMEM((side, rows, 1, width), F32),
+            pltpu.VMEM((rows, 1, width), F32),
+            pltpu.VMEM((rows, 1, width), F32),
+            dma((6,)),
             dma((2,)),
             dma,
             dma((rows,)),
-            dma,
-            dma((rows,)),
+            dma((4,)),
             dma((2,)),
             dma((2,)),
             dma,
             dma((rows,)),
             dma((2,)),
-            dma((2,)),
+            dma((4,)),
         ],
         compiler_params=pltpu.CompilerParams(
-            collective_id=0, has_side_effects=True, vmem_limit_bytes=48 * 1024 * 1024
+            collective_id=0, has_side_effects=True, vmem_limit_bytes=60 * 1024 * 1024
         ),
     )(tokens, router_weight.T, expert_ids.T, down_weight[0], expert_hidden[0], out_grad)
     return down[None], hidden[None], router, gtok

time: 114 us -> 88.5 us (0.78)
  Pallas kernels: 104 us -> 80.8 us
  local copies, waits for them, and re-layouts: 8.52 us -> 6.36 us
    pallas_call x1, Pallas kernels: 104 us -> 80.8 us  [per_device(): pl.pallas_call(functools.partial(kernel, side, cap), out_shape=shapes, in...]
    unnamed x16 -> x4, local copies, waits for them, and re-layouts: 8.52 us -> 6.36 us
where the time goes in v2:
time: 88.5 us; the launch traced here: 87.8 us
  Pallas kernels  80.8 us (91%)
  local copies, waits for them, and re-layouts  6.36 us (7%)
    pallas_call x1, Pallas kernels, per_device(): pl.pallas_call(functools.partial(kernel, side, cap), out_shape=shapes, in...  80.8 us
    unnamed x4, local copies, waits for them, and re-layouts  6.36 us

profile of v2, /device:TPU:1, one launch (start us, length us, event | category | flops | bytes accessed | tf_op | source)
XLA Modules:
  0.0 87.8 jit_solution(5126787597888360971)
XLA Ops:
  0.6 80.8 %shard_map.93 = (f32[256,768]{1,0:T(8,128)}, bf16[96,768]{1,0:T(8,128)(2,1)}, f32[4,64]{1,0:T(4,128)}, bf16[128,256]{1,0:T(8,128)(2,1)}) custom-call(bf16[128,256]{1,0:T(8,128)(2,1)} %tok_any.1, bf16[64,256]{1,0:T(8,128)(2,1)} %bitcast.10, s32[8,128]{1,0:T(8,128)} %bitcast.11, bf16[768,256]{1,0:T(8,128)(2,1)} %bitcast.8, bf16[1536,768]{1,0:T(8,128)(2,1)} %bitcast.6, ...), custom_call_target="tpu_custom_call" | custom-call | tf_op jit(solution)/shard_map/pallas_call | solution.py:387
  81.4 2.1 %copy.14 = f32[1,256,768]{2,1,0:T(8,128)} copy(f32[1,256,768]{2,1,0:T(8,128)} %bitcast.7) | data formatting | bytes 1572864
  83.5 1.6 %copy.15 = bf16[1,96,768]{2,1,0:T(8,128)(2,1)} copy(bf16[1,96,768]{2,1,0:T(8,128)(2,1)} %bitcast.9) | data formatting | bytes 294912
  85.1 1.2 %copy.16 = f32[4,64]{1,0:T(4,128)} copy(f32[4,64]{1,0:T(4,128)} %get-tuple-element.18) | data formatting | bytes 2048
  86.3 1.5 %copy.17 = bf16[128,256]{1,0:T(8,128)(2,1)} copy(bf16[128,256]{1,0:T(8,128)(2,1)} %get-tuple-element.19) | data formatting | bytes 131072

commit v3 on v2

--- a/solution.py
+++ b/solution.py
@@ -113,7 +113,7 @@
     loads = [
         pltpu.make_async_copy(src, dst, load_sem.at[j])
         for j, (src, dst) in enumerate(
-            [(idt_any, idt), (tok_any, tok), (rwt_any, rwt), (grad_any, grad), (w_any, w), (h_any, h)]
+            [(idt_any, idt), (grad_any, grad), (tok_any, tok), (rwt_any, rwt), (w_any, w), (h_any, h)]
         )
     ]
     for load in loads:
@@ -133,8 +133,7 @@
             barrier, inc=1, device_id=((q + i) % edp, e), device_id_type=pl.DeviceIdType.MESH
         )
 
-    for load in loads[:3]:
-        load.wait()
+    loads[0].wait()
     expert = lax.broadcasted_iota(jnp.int32, (ep, count), 0)
     slot = lax.broadcasted_iota(jnp.int32, (side, cap, count), 1).astype(F32)
     lane = lax.broadcasted_iota(jnp.int32, (side, cap, count), 2).astype(F32)
@@ -155,8 +154,6 @@
         spread = jnp.broadcast_to(ranks[:, None, :], (side, cap, count))
         return jnp.where(spread == slot, 1.0, 0.0).astype(F32).reshape(group, count)
 
-    lsend[...] = to_picks(matmul(rwt[...], tok[...], NT))
-    lrecv[q] = lsend[...]
     named = to_experts(jnp.ones((top, count), F32))
     before = (
         lax.broadcasted_iota(jnp.int32, (count, count), 0)
@@ -167,12 +164,8 @@
     )
     rank_s[...] = rank
 
-    loads[3].wait()
+    loads[1].wait()
     pl.semaphore_wait(barrier, ep - 1 + edp - 1)
-
-    @pl.loop(1, edp)
-    def _(i):
-        push(lsend, lrecv.at[q], l_sem.at[0], l_sem.at[1], ((q + i) % edp, e))
 
     def exchange(row, src, dst, send, recv):
         @pl.loop(0, side)
@@ -200,6 +193,15 @@
 
     ahead = min(EARLY, rows)
     pl.loop(0, ahead)(dispatch)
+
+    for load in loads[2:4]:
+        load.wait()
+    lsend[...] = to_picks(matmul(rwt[...], tok[...], NT))
+    lrecv[q] = lsend[...]
+
+    @pl.loop(1, edp)
+    def _(i):
+        push(lsend, lrecv.at[q], l_sem.at[0], l_sem.at[1], ((q + i) % edp, e))
 
     def weigh():
         drain(lrecv.at[pl.ds(0, edp - 1)], l_sem.at[1])

time: 88.5 us -> 88.5 us (level)
  no operation moved by 1% of the time
where the time goes in v3:
time: 88.5 us; the launch traced here: 87.8 us
  Pallas kernels  80.8 us (91%)
  local copies, waits for them, and re-layouts  6.36 us (7%)
    pallas_call x1, Pallas kernels, per_device(): pl.pallas_call(functools.partial(kernel, side, cap), out_shape=shapes, in...  80.8 us
    unnamed x4, local copies, waits for them, and re-layouts  6.36 us

profile of v3, /device:TPU:1, one launch (start us, length us, event | category | flops | bytes accessed | tf_op | source)
XLA Modules:
  0.0 87.8 jit_solution(10926933370306824911)
XLA Ops:
  0.6 80.8 %shard_map.93 = (f32[256,768]{1,0:T(8,128)}, bf16[96,768]{1,0:T(8,128)(2,1)}, f32[4,64]{1,0:T(4,128)}, bf16[128,256]{1,0:T(8,128)(2,1)}) custom-call(bf16[128,256]{1,0:T(8,128)(2,1)} %tok_any.1, bf16[64,256]{1,0:T(8,128)(2,1)} %bitcast.10, s32[8,128]{1,0:T(8,128)} %bitcast.11, bf16[768,256]{1,0:T(8,128)(2,1)} %bitcast.8, bf16[1536,768]{1,0:T(8,128)(2,1)} %bitcast.6, ...), custom_call_target="tpu_custom_call" | custom-call | tf_op jit(solution)/shard_map/pallas_call | solution.py:389
  81.4 2.1 %copy.14 = f32[1,256,768]{2,1,0:T(8,128)} copy(f32[1,256,768]{2,1,0:T(8,128)} %bitcast.7) | data formatting | bytes 1572864
  83.5 1.6 %copy.15 = bf16[1,96,768]{2,1,0:T(8,128)(2,1)} copy(bf16[1,96,768]{2,1,0:T(8,128)(2,1)} %bitcast.9) | data formatting | bytes 294912
  85.1 1.2 %copy.16 = f32[4,64]{1,0:T(4,128)} copy(f32[4,64]{1,0:T(4,128)} %get-tuple-element.18) | data formatting | bytes 2048
  86.3 1.5 %copy.17 = bf16[128,256]{1,0:T(8,128)(2,1)} copy(bf16[128,256]{1,0:T(8,128)(2,1)} %get-tuple-element.19) | data formatting | bytes 131072
